TPU v7x, 32 devices: a whole 2x2x4 slice. The times are simulated.
32 devices in a mesh: mode: 2 (over x), space: 16 (over z, y, core).
Axes of the slice: x: 2, y: 2, z: 4, core: 2. Of those that a mesh axis runs over, the one named last changes fastest.
Arguments:
- mode_fields: bfloat16 [128, 2, 64, 256], P('mode', None, 'space'), may hold values from -6 to 6
- metric: float32 [3, 64, 256], P(None, 'space'), may hold values from 0.5 to 2
- plan: int32 [4, 2], replicated, may hold values from 0 to 1, as said below
Outputs:
- tensor: float32 [4096, 128], P('space', 'mode')
Inputs may be any that keep to these rules, and one draw needn't show every extreme that they name: `plan`: rows 0 and 1 name the advecting blocks, rows 2 and 3 the advected blocks: column 0 a mode group, column 1 a half of its modes (0 or 1). Blocks may repeat.
All inputs are finite; a program needn't handle non-finite values.
Results may differ from a plain program's by a relative error of at most 0.0041.
Values may be sent and summed in bfloat16 or wider, within the bound.
A program may use at most 64 MiB of HBM per device.

v0:
```python
import jax
import jax.numpy as jnp
from jax import lax
from jax.sharding import PartitionSpec as P


def broadcast(block, axis, holder):
    block = jnp.where(lax.axis_index(axis) == holder, block, jnp.zeros_like(block))
    return lax.psum(block, axis)


def with_halo(block, sides, width):
    for axis, dim in sides:
        count = lax.axis_size(axis)
        forward = [(i, i + 1) for i in range(count - 1)]
        backward = [(target, source) for source, target in forward]
        low = lax.ppermute(
            lax.slice_in_dim(block, block.shape[dim] - width, None, axis=dim), axis, forward
        )
        high = lax.ppermute(lax.slice_in_dim(block, 0, width, axis=dim), axis, backward)
        block = jnp.concatenate([low, block, high], axis=dim)
    return block


def stencil(padded, metric):
    widened = padded.astype(jnp.float32)
    along_x = (widened[:, :, 2:, :] - widened[:, :, :-2, :]) * metric[0]
    interior = jnp.pad(widened[:, :, 1:-1, :], ((0, 0), (0, 0), (0, 0), (1, 1)))
    along_y = (interior[:, :, :, 2:] - interior[:, :, :, :-2]) * metric[1]
    return jnp.stack((along_x, along_y), axis=1).astype(jnp.bfloat16)


def advect(column, slopes, weight):
    widened = column.astype(jnp.float32)
    mixed = widened[0] * slopes[:, 0].astype(jnp.float32) + widened[1] * slopes[:, 1].astype(
        jnp.float32
    )
    return (mixed * weight).astype(jnp.bfloat16).reshape(slopes.shape[0], -1)


def body(mode_fields, metric, plan):
    half_size = mode_fields.shape[0] // 2

    def own_block(source_row):
        return lax.dynamic_slice_in_dim(mode_fields, plan[source_row, 1] * half_size, half_size, 0)

    pieces = [
        broadcast(own_block(source_row), "mode", plan[source_row, 0]) for source_row in range(2)
    ]
    movers = jnp.concatenate(pieces, axis=0)
    received = [
        broadcast(own_block(source_row), "mode", plan[source_row, 0]) for source_row in range(2, 4)
    ]
    carried = jnp.concatenate(received, axis=0)
    padded = with_halo(carried, (("space", 2),), 1)
    slopes = stencil(padded, metric)
    test_rows = mode_fields.reshape(mode_fields.shape[0], -1)
    advected_count = slopes.shape[0]
    norm_factor = float(mode_fields.shape[2] * lax.axis_size("space") * mode_fields.shape[3]) ** (
        -0.5
    )

    def project(column):
        advected_field = advect(column, slopes, metric[2])
        return lax.dot_general(
            advected_field, test_rows, (((1,), (1,)), ((), ())), preferred_element_type=jnp.float32
        )

    slot_rows = movers.shape[0] * advected_count // lax.axis_size("space")
    mover_count = slot_rows * lax.axis_size("space") // advected_count
    blocks = lax.map(project, movers, batch_size=min(mover_count, 4))
    return lax.psum_scatter(
        blocks.reshape(slot_rows * lax.axis_size("space"), test_rows.shape[0]) * norm_factor,
        "space",
        scatter_dimension=0,
        tiled=True,
    )


def solution(mesh):
    return jax.shard_map(
        body,
        mesh=mesh,
        in_specs=(P("mode", None, "space", None), P(None, "space", None), P()),
        out_specs=P("space", "mode"),
        check_vma=False,
    )
```

profile of v0, /device:TPU:0, one launch (start us, length us, event | category | flops | bytes accessed | tf_op | source)
XLA Modules:
  0.0 160.0 jit_solution(12218386147194699665)
XLA Ops:
  6.5 1.6 %fusion.15 = (s32[1,1]{0,1:T(1,128)}, s32[1,1]{0,1:T(1,128)}, s32[1,1]{0,1:T(1,128)}, s32[1,1]{0,1:T(1,128)}, s32[1,1]{0,1:T(1,128)}, /*index=5*/s32[1,1]{0,1:T(1,128)}, s32[1,1]{0,1:T(1,128)}, s32[1,1]{0,1:T(1,128)}) fusion(s32[4,2]{0,1:T(2,128)} %param.7), kind=kLoop, calls=%fused_computation.40 | loop fusion | bytes 64 | tf_op jit(solution)/shard_map/slice | solution.py:52
  13.1 2.2 %dynamic-slice_select_fusion = (bf16[32,2,4,256]{3,2,1,0:T(4,128)(2,1)}, bf16[32,2,4,256]{3,2,1,0:T(4,128)(2,1)}, bf16[32,2,4,256]{3,2,1,0:T(4,128)(2,1)}, bf16[32,2,4,256]{3,2,1,0:T(4,128)(2,1)}) fusion(bf16[64,2,4,256]{3,2,1,0:T(4,128)(2,1)} %param.5, s32[]{:T(128)S(6)} %select_n.48, pred[]{:T(512)S(6)} %eq.15, s32[]{:T(128)S(6)} %select_n.45, ...), kind=kLoop, calls=%fused_computation.31 | loop fusion | flops 262144 | bytes 1048596 | tf_op jit(solution)/shard_map/jit(_where)/select_n | solution.py:8
  15.4 1.1 reshape.46
  16.5 30.8 %all-reduce.4.cloned.1.call-done = (bf16[32,2,4,256]{3,2,1,0:T(4,128)(2,1)}, bf16[32,2,4,256]{3,2,1,0:T(4,128)(2,1)}, bf16[32,2,4,256]{3,2,1,0:T(4,128)(2,1)}, bf16[32,2,4,256]{3,2,1,0:T(4,128)(2,1)}) async-done(((bf16[32,2,4,256]{3,2,1,0:T(4,128)(2,1)}, bf16[32,2,4,256]{3,2,1,0:T(4,128)(2,1)}, bf16[32,2,4,256]{3,2,1,0:T(4,128)(2,1)}, bf16[32,2,4,256]{3,2,1,0:T(4,128)(2,1)}), ...) | async-done | bytes 524304 | tf_op jit(solution)/shard_map/psum | solution.py:9
  47.3 0.9 constant_dynamic-update-slice_fusion.1
  48.3 1.0 constant_dynamic-update-slice_fusion
  49.4 1.8 %collective-permute-start = (bf16[64,2,1,256]{3,2,1,0:T(2,128)(2,1)S(1)}, bf16[64,2,1,256]{3,2,1,0:T(2,128)(2,1)S(1)}, u32[]{:S(2)}, u32[]{:S(2)}) collective-permute-start(bf16[64,2,1,256]{3,2,1,0:T(2,128)(2,1)S(1)} %get-tuple-element.66), channel_id=1, source_target_pairs={{0,1},{1,2},{2,3},{3,4},{4,5},{5,6},{6,7},{7,8},{8,9},{9,10},{10,1... | collective-permute-start | bytes 196616 | tf_op jit(solution)/shard_map/ppermute | solution.py:17
  51.2 1.3 collective-permute-start.1
  52.5 1.1 pad_maximum_fusion.1
  53.7 2.0 %collective-permute-done.1 = bf16[64,2,1,256]{3,2,1,0:T(2,128)(2,1)S(1)} collective-permute-done((bf16[64,2,1,256]{3,2,1,0:T(2,128)(2,1)S(1)}, bf16[64,2,1,256]{3,2,1,0:T(2,128)(2,1)S(1)}, u32[]{:S(2)}, u32[]{:S(2)}) %collective-permute-start.1) | collective-permute-done | bytes 65568 | tf_op jit(solution)/shard_map/ppermute | solution.py:20
  55.7 0.4 maximum_convert_fusion
  56.4 0.6 fusion.13
  57.4 31.7 %while.10 = (s32[]{:T(128)}, f32[16,4,64,64]{3,2,1,0:T(8,128)}, bf16[16,4,2,4,256]{4,3,2,1,0:T(4,128)(2,1)S(1)}, bf16[64,2,2,4,256]{4,3,2,0,1:T(4,128)(2,1)S(1)}...) while((s32[]{:T(128)}, f32[16,4,64,64]{3,2,1,0:T(8,128)}, ...), condition=%wide.region_5.6_spmd, body=%wide.region_4.5_spmd.sunk | while | flops 70000640 | bytes 5567057 | solution.py:71
  58.2 1.1 fusion.21
  60.2 1.1 fusion.21
  62.2 1.1 fusion.21
  64.2 1.1 fusion.21
  66.2 1.1 fusion.21
  68.1 1.1 fusion.21
  70.1 1.1 fusion.21
  72.1 1.1 fusion.21
  74.1 1.1 fusion.21
  76.1 1.1 fusion.21
  78.0 1.1 fusion.21
  80.0 1.1 fusion.21
  82.0 1.1 fusion.21
  84.0 1.1 fusion.21
  85.9 1.1 fusion.21
  87.9 1.1 fusion.21
  89.1 1.8 %broadcast_multiply_fusion = f32[16,4,64,64]{3,2,1,0:T(8,128)S(1)} fusion(f32[16,4,64,64]{3,2,1,0:T(8,128)} %get-tuple-element.37), kind=kLoop, calls=%fused_computation.17 | loop fusion | flops 262144 | bytes 2097152 | tf_op jit(solution)/shard_map/mul | solution.py:73
  90.8 1.6 copy.7
  92.4 60.7 %reduce-scatter.2.cloned.1.call-done = f32[256,64]{0,1:T(8,128)} async-done(((f32[4096,64]{0,1:T(8,128)}), f32[256,64]{0,1:T(8,128)}) %reduce-scatter.2.cloned.1.call-update) | async-done | bytes 65552 | tf_op jit(solution)/shard_map/reduce_scatter | solution.py:72
  (204 shorter events, 13.4 us)
Async XLA Ops:
  6.5 10.0 %copy-start = (f32[3,4,256]{2,1,0:T(4,128)S(1)}, f32[3,4,256]{2,1,0:T(4,128)}, u32[]{:S(2)}) copy-start(f32[3,4,256]{2,1,0:T(4,128)} %param.6) | copy-start | bytes 36868
  6.5 40.8 %all-reduce.4.cloned.1.call-start = ((), (), s32[]{:S(2)}) async-start(), calls=%async_computation.2 | async-start | bytes 1048576 | tf_op jit(solution)/shard_map/psum | solution.py:9
  15.3 137.8 %reduce-scatter.2.cloned.1.call-start = ((), (), s32[]{:S(2)}) async-start(), calls=%async_computation.1 | async-start | bytes 1114112 | tf_op jit(solution)/shard_map/reduce_scatter | solution.py:72
  49.4 4.2 %collective-permute-start = (bf16[64,2,1,256]{3,2,1,0:T(2,128)(2,1)S(1)}, bf16[64,2,1,256]{3,2,1,0:T(2,128)(2,1)S(1)}, u32[]{:S(2)}, u32[]{:S(2)}) collective-permute-start(bf16[64,2,1,256]{3,2,1,0:T(2,128)(2,1)S(1)} %get-tuple-element.66), channel_id=1, source_target_pairs={{0,1},{1,2},{2,3},{3,4},{4,5},{5,6},{6,7},{7,8},{8,9},{9,10},{10,1... | collective-permute-start | bytes 196616 | tf_op jit(solution)/shard_map/ppermute | solution.py:17
  51.2 4.5 %collective-permute-start.1 = (bf16[64,2,1,256]{3,2,1,0:T(2,128)(2,1)S(1)}, bf16[64,2,1,256]{3,2,1,0:T(2,128)(2,1)S(1)}, u32[]{:S(2)}, u32[]{:S(2)}) collective-permute-start(bf16[64,2,1,256]{3,2,1,0:T(2,128)(2,1)S(1)} %get-tuple-element.67), channel_id=1, source_target_pairs={{1,0},{2,1},{3,2},{4,3},{5,4},{6,5},{7,6},{8,7},{9,8},{10,9},{11,1... | collective-permute-start | bytes 196616 | tf_op jit(solution)/shard_map/ppermute | solution.py:20
Sparse Core Ops, SparseCore 0:
  15.4 31.8 all-reduce.3
  92.5 60.5 reduce-scatter.1
where the time goes:
time: 160 us
  waiting for transfers between devices  93.6 us (58%)
  between operations  18.4 us (11%)
  matrix products  18.1 us (11%)
  local copies, waits for them, and re-layouts  16.6 us (10%)
  other arithmetic  9.13 us (6%)
  starting transfers between devices  3.09 us (2%)
    reduce_scatter x1, waiting for transfers between devices, body(): lax.psum_scatter(blocks.reshape(slot_rows * lax.axis_size('space'), test_...  60.7 us
    psum x1, waiting for transfers between devices, broadcast(): return lax.psum(block, axis)  30.8 us
    dot_general x16, matrix products, project(): lax.dot_general(advected_field, test_rows, (((1,), (1,)), ((), ())), pref...  18.1 us
    convert_element_type x16, local copies, waits for them, and re-layouts, advect(): slopes[:, 1].astype(jnp.float32)  4.35 us
    convert_element_type x16, local copies, waits for them, and re-layouts, advect(): slopes[:, 0].astype(jnp.float32)  4.35 us
  transfers between devices with their start and end apart: 4, of which 3 were waited for; matrix products, arithmetic and copies ran while one was open for 1% of the time, Pallas kernels for 0%

commit v1 on v0

v1 whole, which is shorter than its diff:
```python
import functools

import jax
import jax.numpy as jnp
from jax import lax
from jax.experimental import pallas as pl
from jax.experimental.pallas import tpu as pltpu
from jax.sharding import PartitionSpec as P

MESH = pl.DeviceIdType.MESH
F32 = jnp.float32
BF16 = jnp.bfloat16


def kernel(
    n_mode, n, norm_factor,
    x_ref, metric_ref, plan_ref, out_ref,
    fields, slopes, movers, keep, send1, recv1, send2, recv2, send3, recv3,
    x_send, x_recv, h_send, h_recv, s1_send, s1_recv, s2_send, s2_recv, s3_send, s3_recv,
):
    R, _, half, width = x_ref.shape
    modes = 2 * half
    L = metric_ref.shape[2]
    C = width // L
    nq, nz = n // 2, n // 4
    jb = movers.shape[3]

    me = lax.axis_index("mode")
    s = lax.axis_index("space")
    core = lax.rem(s, 2)
    pair = s // 2
    y = lax.rem(pair, 2)
    z = pair // 2
    twin = s + 1 - 2 * core
    across = s + 2 - 4 * y
    has_left = s > 0
    has_right = s < n - 1
    has_other = ((core == 1) & has_right) | ((core == 0) & has_left)
    other = jnp.clip(s + 2 * core - 1, 0, n - 1)

    def along(step):
        return (lax.rem(z + step, nz) * 2 + y) * 2 + core

    barrier = pltpu.get_barrier_semaphore()

    def greet(device):
        pl.semaphore_signal(barrier, inc=1, device_id=device, device_id_type=MESH)

    for d in range(1, n_mode):
        greet((lax.rem(me + d, n_mode), s))
    greet((me, twin))
    greet((me, across))
    for step in range(1, nz):
        greet((me, along(step)))

    @pl.when(has_other)
    def _():
        greet((me, other))

    greeted = (n_mode - 1) + 2 + (nz - 1)
    pl.semaphore_wait(barrier, jnp.where(has_other, greeted + 1, greeted))

    def remote(src, dst, send, recv, device):
        return pltpu.make_async_remote_copy(
            src_ref=src, dst_ref=dst, send_sem=send, recv_sem=recv,
            device_id=device, device_id_type=MESH,
        )

    def spread(d, piece):
        peer = (lax.rem(me + d, n_mode), s)
        rows = ((0, 1), (R - 1, 1), (1, R - 2))[piece]
        return remote(
            x_ref.at[pl.ds(rows[0], rows[1])],
            fields.at[me, pl.ds(1 + rows[0], rows[1])],
            x_send.at[d, piece], x_recv.at[d, piece], peer,
        )

    def halo(d, side):
        group = lax.rem(me + n_mode - d, n_mode)
        if d == 0:
            src = x_ref.at[0 if side == 0 else R - 1]
        else:
            src = fields.at[group, 1 if side == 0 else R]
        target = (me, jnp.maximum(s - 1, 0)) if side == 0 else (me, jnp.minimum(s + 1, n - 1))
        return remote(
            src, fields.at[group, R + 1 if side == 0 else 0],
            h_send.at[d, side], h_recv.at[d, side], target,
        )

    for piece in range(3):
        for d in range(1, n_mode):
            spread(d, piece).start()

    def start_halo(d):
        @pl.when(has_left)
        def _():
            halo(d, 0).start()

        @pl.when(has_right)
        def _():
            halo(d, 1).start()

    start_halo(0)
    for r in range(R):
        fields[me, 1 + r] = x_ref[r]

    @pl.when(jnp.logical_not(has_left))
    def _():
        for g in range(n_mode):
            fields[g, 0] = jnp.zeros_like(fields[g, 0])

    @pl.when(jnp.logical_not(has_right))
    def _():
        for g in range(n_mode):
            fields[g, R + 1] = jnp.zeros_like(fields[g, R + 1])

    for d in range(1, n_mode):
        spread(d, 0).wait_recv()
        spread(d, 1).wait_recv()
        start_halo(d)
    for d in range(1, n_mode):
        spread(d, 2).wait_recv()
    for d in range(n_mode):
        @pl.when(has_right)
        def _():
            halo(d, 0).wait_recv()

        @pl.when(has_left)
        def _():
            halo(d, 1).wait_recv()

    lane = lax.rem(lax.broadcasted_iota(jnp.int32, (half, width), 1), L)
    for b in range(2):
        owner, which = plan_ref[b, 0], plan_ref[b, 1]
        for r in range(R):
            block = fields[owner, 1 + r, which].astype(F32)
            weight = metric_ref[2, r : r + 1, :]
            for c in range(2):
                scaled = block[:, c * L : (c + 1) * L] * weight
                movers[c, r, pl.ds(b * (half // jb), half // jb)] = scaled.reshape(
                    half // jb, jb, L
                )
    for b in range(2):
        owner, which = plan_ref[2 + b, 0], plan_ref[2 + b, 1]
        for r in range(R):
            low = fields[owner, r, which].astype(F32)
            mid = fields[owner, r + 1, which].astype(F32)
            high = fields[owner, r + 2, which].astype(F32)
            first = jnp.concatenate([metric_ref[0, r : r + 1, :]] * C, axis=1)
            second = jnp.concatenate([metric_ref[1, r : r + 1, :]] * C, axis=1)
            after = jnp.where(lane == L - 1, 0.0, pltpu.roll(mid, width - 1, 1))
            before = jnp.where(lane == 0, 0.0, pltpu.roll(mid, 1, 1))
            place = slice(b * half, (b + 1) * half)
            slopes[0, r, place, :] = ((high - low) * first).astype(BF16).astype(F32)
            slopes[1, r, place, :] = ((after - before) * second).astype(BF16).astype(F32)

    def project(q):
        total = None
        for r in range(R):
            rows = []
            for j in range(jb):
                m0 = movers[0, r, q, j : j + 1, :]
                m1 = movers[1, r, q, j : j + 1, :]
                parts = []
                for c in range(C):
                    lanes = slice(c * L, (c + 1) * L)
                    mixed = m0 * slopes[0, r, :, lanes] + m1 * slopes[1, r, :, lanes]
                    parts.append(mixed.astype(BF16))
                rows.append(jnp.concatenate(parts, axis=1))
            part = lax.dot_general(
                jnp.concatenate(rows, axis=0), x_ref[r].reshape(modes, width),
                (((1,), (1,)), ((), ())), preferred_element_type=F32,
            )
            total = part if total is None else total + part
        return total

    def pack(rows):
        h = rows.shape[0] // 2
        return jnp.concatenate([rows[:h], rows[h:]], axis=1)

    def to_twin(it):
        return remote(
            send1.at[it], recv1.at[it], s1_send.at[it], s1_recv.at[it], (me, twin)
        )

    def to_across(t):
        return remote(
            send2.at[t], recv2.at[t], s2_send.at[t], s2_recv.at[t], (me, across)
        )

    def to_along(t):
        return remote(
            send3.at[t], recv3.at[t], s3_send.at[t], s3_recv.at[t], (me, along(t + 1))
        )

    def gathered(it):
        to_twin(it).wait_recv()
        return keep[it] + recv1[it].astype(F32)

    def step(it, carry):
        t = lax.rem(it, nz)
        column = jnp.where(it < nz, 1 - y, y)
        q = lax.rem(z + 1 + t, nz) * 2 + column
        total = project(q)
        rows = total.shape[0] // 2
        low, high = pack(total[:rows]), pack(total[rows:])
        keep[it] = jnp.where(core == 0, low, high)
        send1[it] = jnp.where(core == 0, high, low).astype(BF16)
        to_twin(it).start()

        @pl.when((it >= 1) & (it <= nz))
        def _():
            t = it - 1
            send2[t] = gathered(it - 1).astype(BF16)
            to_across(t).start()

        @pl.when(it > nz)
        def _():
            t = it - 1 - nz
            value = gathered(it - 1)
            to_across(t).wait_recv()
            send3[t] = (value + recv2[t].astype(F32)).astype(BF16)
            to_along(t).start()

        return carry

    lax.fori_loop(0, nq, step, 0)

    value = gathered(nq - 1)
    to_across(nz - 1).wait_recv()
    value = value + recv2[nz - 1].astype(F32)
    for t in range(nz - 1):
        to_along(t).wait_recv()
        value = value + recv3[t].astype(F32)
    value = value * norm_factor
    h = value.shape[0]
    out_ref[pl.ds(0, h), :] = value[:, :modes]
    out_ref[pl.ds(h, h), :] = value[:, modes:]

    for d in range(1, n_mode):
        for piece in range(3):
            spread(d, piece).wait_send()
    for d in range(n_mode):
        @pl.when(has_left)
        def _():
            halo(d, 0).wait_send()

        @pl.when(has_right)
        def _():
            halo(d, 1).wait_send()
    for it in range(nq):
        to_twin(it).wait_send()
    for t in range(nz):
        to_across(t).wait_send()
    for t in range(nz - 1):
        to_along(t).wait_send()


def body(mode_fields, metric, plan):
    n_mode, n = lax.axis_size("mode"), lax.axis_size("space")
    modes, C, R, L = mode_fields.shape
    half, width = modes // 2, C * L
    norm_factor = float(R * n * L) ** (-0.5)
    out_rows = modes * modes // n
    h = out_rows // 2
    nq, nz = n // 2, n // 4
    jb = modes // nq
    x = mode_fields.transpose(2, 0, 1, 3).reshape(R, 2, half, width)
    dma = pltpu.SemaphoreType.DMA
    return pl.pallas_call(
        functools.partial(kernel, n_mode, n, norm_factor),
        out_shape=jax.ShapeDtypeStruct((out_rows, modes), F32),
        in_specs=[
            pl.BlockSpec(memory_space=pltpu.VMEM),
            pl.BlockSpec(memory_space=pltpu.VMEM),
            pl.BlockSpec(memory_space=pltpu.SMEM),
        ],
        out_specs=pl.BlockSpec(memory_space=pltpu.VMEM),
        scratch_shapes=[
            pltpu.VMEM((n_mode, R + 2, 2, half, width), BF16),
            pltpu.VMEM((2, R, modes, width), F32),
            pltpu.VMEM((2, R, nq, jb, L), F32),
            pltpu.VMEM((nq, h, 2 * modes), F32),
            pltpu.VMEM((nq, h, 2 * modes), BF16),
            pltpu.VMEM((nq, h, 2 * modes), BF16),
            pltpu.VMEM((nz, h, 2 * modes), BF16),
            pltpu.VMEM((nz, h, 2 * modes), BF16),
            pltpu.VMEM((nz, h, 2 * modes), BF16),
            pltpu.VMEM((nz, h, 2 * modes), BF16),
            dma((n_mode, 3)),
            dma((n_mode, 3)),
            dma((n_mode, 2)),
            dma((n_mode, 2)),
            dma((nq,)),
            dma((nq,)),
            dma((nz,)),
            dma((nz,)),
            dma((nz,)),
            dma((nz,)),
        ],
        compiler_params=pltpu.CompilerParams(
            collective_id=0, has_side_effects=True, vmem_limit_bytes=40 * 1024 * 1024
        ),
    )(x, metric, plan)


def solution(mesh):
    return jax.shard_map(
        body,
        mesh=mesh,
        in_specs=(P("mode", None, "space", None), P(None, "space", None), P()),
        out_specs=P("space", "mode"),
        check_vma=False,
    )
```

time: 160 us -> 28.3 us (0.18)
  waiting for transfers between devices: 93.6 us -> 0 us
  Pallas kernels: 0 us -> 25.5 us
  between operations: 18.4 us -> 0.04 us
  matrix products: 18.1 us -> 0 us
  local copies, waits for them, and re-layouts: 16.6 us -> 2.62 us
  other arithmetic: 9.13 us -> 0 us
  starting transfers between devices: 3.09 us -> 0 us
    reduce_scatter x1 -> x0, waiting for transfers between devices: 60.7 us -> none  [body(): lax.psum_scatter(blocks.reshape(slot_rows * lax.axis_size('space'), test_...]
    psum x1 -> x0, waiting for transfers between devices: 30.8 us -> none  [broadcast(): return lax.psum(block, axis)]
    pallas_call x0 -> x1, Pallas kernels: none -> 25.5 us  [body(): pl.pallas_call(functools.partial(kernel, n_mode, n, norm_factor), out_sha...]
    dot_general x16 -> x0, matrix products: 18.1 us -> none  [project(): lax.dot_general(advected_field, test_rows, (((1,), (1,)), ((), ())), pref...]
    convert_element_type x32 -> x0, local copies, waits for them, and re-layouts: 8.69 us -> none  [the longest x16 4.35 us: advect(): slopes[:, 1].astype(jnp.float32)]
    ppermute x2 -> x0, starting transfers between devices: 3.04 us -> none  [the longest x1 1.75 us: with_halo(): lax.ppermute(lax.slice_in_dim(block, block.shape[dim] - width, None, axis...]
    mul x98 -> x0, local copies, waits for them, and re-layouts: 2.88 us -> none  [the longest x1 1.56 us: body(): blocks.reshape(slot_rows * lax.axis_size('space'), test_rows.shape[0])]
    convert_element_type x33 -> x0, other arithmetic: 2.77 us -> none  [the longest x16 2.29 us: advect(): slopes[:, 0].astype(jnp.float32)]
  transfers between devices with their start and end apart: 4 -> 0, of which waited for: 3 -> 0; matrix products, arithmetic and copies ran while one was open for 1% -> 0% of each run, Pallas kernels for 0% -> 0%
where the time goes in v1:
time: 28.3 us; the launch traced here: 28.2 us
  Pallas kernels  25.5 us (90%)
  local copies, waits for them, and re-layouts  2.62 us (9%)
    pallas_call x1, Pallas kernels, body(): pl.pallas_call(functools.partial(kernel, n_mode, n, norm_factor), out_sha...  25.5 us
    transpose x1, local copies, waits for them, and re-layouts, body(): x = mode_fields.transpose(2, 0, 1, 3).reshape(R, 2, half, width)  1.15 us
    pallas_call x1, local copies, waits for them, and re-layouts, body(): pl.pallas_call(functools.partial(kernel, n_mode, n, norm_factor), out_sha...  0.71 us
    unnamed x5, local copies, waits for them, and re-layouts  0.58 us

profile of v1, /device:TPU:0, one launch (start us, length us, event | category | flops | bytes accessed | tf_op | source)
XLA Modules:
  0.0 28.2 jit_solution(5915154974982542768)
XLA Ops:
  0.0 1.2 %copy.4 = bf16[4,64,2,256]{3,2,1,0:T(2,128)(2,1)S(1)} copy(bf16[4,64,2,256]{3,0,2,1:T(4,128)(2,1)} %bitcast.1) | data formatting | bytes 524288 | tf_op jit(solution)/shard_map/transpose | solution.py:268
  1.2 0.0 copy-start.1
  1.2 0.0 copy-start
  1.2 0.2 reshape.3.x_ref
  1.4 0.5 %copy-done.1 = s32[4,2]{0,1:T(2,128)S(1)} copy-done((s32[4,2]{0,1:T(2,128)S(1)}, s32[4,2]{0,1:T(2,128)}, u32[]{:S(2)}) %copy-start.1) | copy-done | bytes 56
  1.8 0.1 copy.5.plan_ref
  1.9 0.0 copy-done
  1.9 25.5 %shard_map.37 = f32[256,64]{1,0:T(8,128)S(1)} custom-call(bf16[4,2,32,512]{3,2,1,0:T(8,128)(2,1)S(1)} %reshape.3.x_ref, f32[3,4,256]{2,1,0:T(4,128)S(1)} %copy-done, s32[4,2]{1,0:T(4,128)S(1)} %copy.5.plan_ref), custom_call_target="tpu_custom_call" | custom-call | tf_op jit(solution)/shard_map/pallas_call | solution.py:270
  27.4 0.7 %copy.6 = f32[256,64]{0,1:T(8,128)} copy(f32[256,64]{1,0:T(8,128)S(1)} %shard_map.37) | data formatting | bytes 131072 | tf_op jit(solution)/shard_map/pallas_call | solution.py:270
Async XLA Ops:
  1.2 0.7 %copy-start.1 = (s32[4,2]{0,1:T(2,128)S(1)}, s32[4,2]{0,1:T(2,128)}, u32[]{:S(2)}) copy-start(s32[4,2]{0,1:T(2,128)} %param.5) | copy-start | bytes 100
  1.2 0.8 %copy-start = (f32[3,4,256]{2,1,0:T(4,128)S(1)}, f32[3,4,256]{2,1,0:T(4,128)}, u32[]{:S(2)}) copy-start(f32[3,4,256]{2,1,0:T(4,128)} %metric_ref.1) | copy-start | bytes 36868

commit v2 on v1

--- a/solution.py
+++ b/solution.py
@@ -13,13 +13,14 @@
 
 
 def kernel(
-    n_mode, n, norm_factor,
+    n_mode, n, parts, norm_factor,
     x_ref, metric_ref, plan_ref, out_ref,
-    fields, slopes, movers, keep, send1, recv1, send2, recv2, send3, recv3,
+    fields, weights, slopes, movers, keep, send1, recv1, send2, recv2, send3, recv3,
     x_send, x_recv, h_send, h_recv, s1_send, s1_recv, s2_send, s2_recv, s3_send, s3_recv,
 ):
     R, _, half, width = x_ref.shape
     modes = 2 * half
+    own = modes // parts
     L = metric_ref.shape[2]
     C = width // L
     nq, nz = n // 2, n // 4
@@ -51,13 +52,14 @@
     greet((me, twin))
     greet((me, across))
     for step in range(1, nz):
-        greet((me, along(step)))
+        for e in range(parts):
+            greet((lax.rem(me + e, n_mode), along(step)))
 
     @pl.when(has_other)
     def _():
         greet((me, other))
 
-    greeted = (n_mode - 1) + 2 + (nz - 1)
+    greeted = (n_mode - 1) + 2 + parts * (nz - 1)
     pl.semaphore_wait(barrier, jnp.where(has_other, greeted + 1, greeted))
 
     def remote(src, dst, send, recv, device):
@@ -131,7 +133,7 @@
 
     lane = lax.rem(lax.broadcasted_iota(jnp.int32, (half, width), 1), L)
     for b in range(2):
-        owner, which = plan_ref[b, 0], plan_ref[b, 1]
+        owner, which = plan_ref[0, b], plan_ref[1, b]
         for r in range(R):
             block = fields[owner, 1 + r, which].astype(F32)
             weight = metric_ref[2, r : r + 1, :]
@@ -140,8 +142,9 @@
                 movers[c, r, pl.ds(b * (half // jb), half // jb)] = scaled.reshape(
                     half // jb, jb, L
                 )
-    for b in range(2):
-        owner, which = plan_ref[2 + b, 0], plan_ref[2 + b, 1]
+    for b in range(2 // parts):
+        source = 2 + b if parts == 1 else 2 + me
+        owner, which = plan_ref[0, source], plan_ref[1, source]
         for r in range(R):
             low = fields[owner, r, which].astype(F32)
             mid = fields[owner, r + 1, which].astype(F32)
@@ -153,26 +156,41 @@
             place = slice(b * half, (b + 1) * half)
             slopes[0, r, place, :] = ((high - low) * first).astype(BF16).astype(F32)
             slopes[1, r, place, :] = ((after - before) * second).astype(BF16).astype(F32)
+    for r in range(R):
+        if parts == 1:
+            tests = x_ref[r].reshape(modes, width)
+        else:
+            tests = jnp.concatenate(
+                [fields[g, 1 + r].reshape(modes, width) for g in range(n_mode)], axis=0
+            )
+        weights[r] = tests.T
+
+    tile = 16
 
     def project(q):
         total = None
         for r in range(R):
+            m = [
+                [jnp.broadcast_to(movers[d, r, q, j : j + 1, :], (tile, L)) for j in range(jb)]
+                for d in range(2)
+            ]
             rows = []
-            for j in range(jb):
-                m0 = movers[0, r, q, j : j + 1, :]
-                m1 = movers[1, r, q, j : j + 1, :]
-                parts = []
+            for k in range(0, own, tile):
+                parted = [[] for _ in range(jb)]
                 for c in range(C):
                     lanes = slice(c * L, (c + 1) * L)
-                    mixed = m0 * slopes[0, r, :, lanes] + m1 * slopes[1, r, :, lanes]
-                    parts.append(mixed.astype(BF16))
-                rows.append(jnp.concatenate(parts, axis=1))
-            part = lax.dot_general(
-                jnp.concatenate(rows, axis=0), x_ref[r].reshape(modes, width),
-                (((1,), (1,)), ((), ())), preferred_element_type=F32,
+                    s0 = slopes[0, r, k : k + tile, lanes]
+                    s1 = slopes[1, r, k : k + tile, lanes]
+                    for j in range(jb):
+                        parted[j].append((m[0][j] * s0 + m[1][j] * s1).astype(BF16))
+                rows += [jnp.concatenate(parted[j], axis=1) for j in range(jb)]
+            part = jnp.dot(
+                jnp.concatenate(rows, axis=0), weights[r], preferred_element_type=F32
             )
             total = part if total is None else total + part
-        return total
+        order = [total[(k * jb + j) * tile : (k * jb + j + 1) * tile]
+                 for j in range(jb) for k in range(own // tile)]
+        return jnp.concatenate(order, axis=0)
 
     def pack(rows):
         h = rows.shape[0] // 2
@@ -188,10 +206,17 @@
             send2.at[t], recv2.at[t], s2_send.at[t], s2_recv.at[t], (me, across)
         )
 
-    def to_along(t):
-        return remote(
-            send3.at[t], recv3.at[t], s3_send.at[t], s3_recv.at[t], (me, along(t + 1))
-        )
+    def to_along(t, e):
+        return remote(
+            send3.at[t, e], recv3.at[t, e], s3_send.at[t, e], s3_recv.at[t, e],
+            (lax.rem(me + e, n_mode), along(t + 1)),
+        )
+
+    def columns(value):
+        if parts == 1:
+            return [value]
+        low, high = pack(value[:, :modes]), pack(value[:, modes:])
+        return [jnp.where(me == 0, low, high), jnp.where(me == 0, high, low)]
 
     def gathered(it):
         to_twin(it).wait_recv()
@@ -203,7 +228,9 @@
         q = lax.rem(z + 1 + t, nz) * 2 + column
         total = project(q)
         rows = total.shape[0] // 2
-        low, high = pack(total[:rows]), pack(total[rows:])
+        low, high = total[:rows], total[rows:]
+        if parts == 1:
+            low, high = pack(low), pack(high)
         keep[it] = jnp.where(core == 0, low, high)
         send1[it] = jnp.where(core == 0, high, low).astype(BF16)
         to_twin(it).start()
@@ -219,8 +246,9 @@
             t = it - 1 - nz
             value = gathered(it - 1)
             to_across(t).wait_recv()
-            send3[t] = (value + recv2[t].astype(F32)).astype(BF16)
-            to_along(t).start()
+            for e, piece in enumerate(columns(value + recv2[t].astype(F32))):
+                send3[t, e] = piece.astype(BF16)
+                to_along(t, e).start()
 
         return carry
 
@@ -228,14 +256,28 @@
 
     value = gathered(nq - 1)
     to_across(nz - 1).wait_recv()
-    value = value + recv2[nz - 1].astype(F32)
-    for t in range(nz - 1):
-        to_along(t).wait_recv()
-        value = value + recv3[t].astype(F32)
-    value = value * norm_factor
-    h = value.shape[0]
-    out_ref[pl.ds(0, h), :] = value[:, :modes]
-    out_ref[pl.ds(h, h), :] = value[:, modes:]
+    pieces = columns(value + recv2[nz - 1].astype(F32))
+    if parts == 2:
+        send3[nz - 1, 1] = pieces[1].astype(BF16)
+        to_along(nz - 1, 1).start()
+    for e in range(parts):
+        value = pieces[0] if e == 0 else None
+        for t in range(nz if e else nz - 1):
+            to_along(t, e).wait_recv()
+            got = recv3[t, e].astype(F32)
+            value = got if value is None else value + got
+        value = value * norm_factor
+        halves = [value[:, :modes], value[:, modes:]]
+        if parts == 1:
+            h = value.shape[0]
+            out_ref[pl.ds(0, h), :] = halves[0]
+            out_ref[pl.ds(h, h), :] = halves[1]
+        else:
+            value = jnp.concatenate(halves, axis=0)
+            column = me if e == 0 else 1 - me
+            for j in range(value.shape[0] // own):
+                start = pl.multiple_of(j * modes + column * own, own)
+                out_ref[pl.ds(start, own), :] = value[j * own : (j + 1) * own]
 
     for d in range(1, n_mode):
         for piece in range(3):
@@ -252,8 +294,10 @@
         to_twin(it).wait_send()
     for t in range(nz):
         to_across(t).wait_send()
-    for t in range(nz - 1):
-        to_along(t).wait_send()
+    for t in range(nz):
+        for e in range(parts):
+            if t < nz - 1 or e > 0:
+                to_along(t, e).wait_send()
 
 
 def body(mode_fields, metric, plan):
@@ -265,10 +309,11 @@
     h = out_rows // 2
     nq, nz = n // 2, n // 4
     jb = modes // nq
+    parts = 2 if n_mode == 2 else 1
     x = mode_fields.transpose(2, 0, 1, 3).reshape(R, 2, half, width)
     dma = pltpu.SemaphoreType.DMA
     return pl.pallas_call(
-        functools.partial(kernel, n_mode, n, norm_factor),
+        functools.partial(kernel, n_mode, n, parts, norm_factor),
         out_shape=jax.ShapeDtypeStruct((out_rows, modes), F32),
         in_specs=[
             pl.BlockSpec(memory_space=pltpu.VMEM),
@@ -278,15 +323,16 @@
         out_specs=pl.BlockSpec(memory_space=pltpu.VMEM),
         scratch_shapes=[
             pltpu.VMEM((n_mode, R + 2, 2, half, width), BF16),
-            pltpu.VMEM((2, R, modes, width), F32),
+            pltpu.VMEM((R, width, modes * parts), BF16),
+            pltpu.VMEM((2, R, modes // parts, width), F32),
             pltpu.VMEM((2, R, nq, jb, L), F32),
             pltpu.VMEM((nq, h, 2 * modes), F32),
             pltpu.VMEM((nq, h, 2 * modes), BF16),
             pltpu.VMEM((nq, h, 2 * modes), BF16),
             pltpu.VMEM((nz, h, 2 * modes), BF16),
             pltpu.VMEM((nz, h, 2 * modes), BF16),
-            pltpu.VMEM((nz, h, 2 * modes), BF16),
-            pltpu.VMEM((nz, h, 2 * modes), BF16),
+            pltpu.VMEM((nz, parts, h // parts, 2 * modes), BF16),
+            pltpu.VMEM((nz, parts, h // parts, 2 * modes), BF16),
             dma((n_mode, 3)),
             dma((n_mode, 3)),
             dma((n_mode, 2)),
@@ -295,13 +341,13 @@
             dma((nq,)),
             dma((nz,)),
             dma((nz,)),
-            dma((nz,)),
-            dma((nz,)),
+            dma((nz, parts)),
+            dma((nz, parts)),
         ],
         compiler_params=pltpu.CompilerParams(
             collective_id=0, has_side_effects=True, vmem_limit_bytes=40 * 1024 * 1024
         ),
-    )(x, metric, plan)
+    )(x, metric, plan.T)
 
 
 def solution(mesh):

time: 28.3 us -> 28.2 us (level)
    unnamed x5 -> x4, local copies, waits for them, and re-layouts: 0.58 us -> 0.52 us
where the time goes in v2:
time: 28.2 us; the launch traced here: 28 us
  Pallas kernels  25.4 us (90%)
  local copies, waits for them, and re-layouts  2.56 us (9%)
    pallas_call x1, Pallas kernels, body(): pl.pallas_call(functools.partial(kernel, n_mode, n, parts, norm_factor),...  25.4 us
    transpose x1, local copies, waits for them, and re-layouts, body(): x = mode_fields.transpose(2, 0, 1, 3).reshape(R, 2, half, width)  1.15 us
    pallas_call x1, local copies, waits for them, and re-layouts, body(): pl.pallas_call(functools.partial(kernel, n_mode, n, parts, norm_factor),...  0.71 us

profile of v2, /device:TPU:0, one launch (start us, length us, event | category | flops | bytes accessed | tf_op | source)
XLA Modules:
  0.0 28.0 jit_solution(592205741806282721)
XLA Ops:
  0.0 1.2 %copy.4 = bf16[4,64,2,256]{3,2,1,0:T(2,128)(2,1)S(1)} copy(bf16[4,64,2,256]{3,0,2,1:T(4,128)(2,1)} %bitcast.3) | data formatting | bytes 524288 | tf_op jit(solution)/shard_map/transpose | solution.py:313
  1.2 0.0 copy-start
  1.2 0.0 copy-start.1
  1.2 0.2 reshape.3.x_ref
  1.4 0.5 %copy-done = f32[3,4,256]{2,1,0:T(4,128)S(1)} copy-done((f32[3,4,256]{2,1,0:T(4,128)S(1)}, f32[3,4,256]{2,1,0:T(4,128)}, u32[]{:S(2)}) %copy-start) | copy-done | bytes 12312
  1.9 0.0 copy-done.1
  1.9 25.4 %shard_map.37 = f32[256,64]{1,0:T(8,128)S(1)} custom-call(bf16[4,2,32,512]{3,2,1,0:T(8,128)(2,1)S(1)} %reshape.3.x_ref, f32[3,4,256]{2,1,0:T(4,128)S(1)} %copy-done, s32[2,4]{1,0:T(2,128)S(1)} %bitcast.2), custom_call_target="tpu_custom_call" | custom-call | tf_op jit(solution)/shard_map/pallas_call | solution.py:315
  27.3 0.7 %copy.5 = f32[256,64]{0,1:T(8,128)} copy(f32[256,64]{1,0:T(8,128)S(1)} %shard_map.37) | data formatting | bytes 131072 | tf_op jit(solution)/shard_map/pallas_call | solution.py:315
Async XLA Ops:
  1.2 0.7 %copy-start = (f32[3,4,256]{2,1,0:T(4,128)S(1)}, f32[3,4,256]{2,1,0:T(4,128)}, u32[]{:S(2)}) copy-start(f32[3,4,256]{2,1,0:T(4,128)} %metric_ref.1) | copy-start | bytes 36868
  1.2 0.7 %copy-start.1 = (s32[4,2]{0,1:T(2,128)S(1)}, s32[4,2]{0,1:T(2,128)}, u32[]{:S(2)}) copy-start(s32[4,2]{0,1:T(2,128)} %param.5) | copy-start | bytes 100

commit v3 on v2

--- a/solution.py
+++ b/solution.py
@@ -14,9 +14,9 @@
 
 def kernel(
     n_mode, n, parts, norm_factor,
-    x_ref, metric_ref, plan_ref, out_ref,
-    fields, weights, slopes, movers, keep, send1, recv1, send2, recv2, send3, recv3,
-    x_send, x_recv, h_send, h_recv, s1_send, s1_recv, s2_send, s2_recv, s3_send, s3_recv,
+    x_ref, metric_hbm, plan_hbm, out_ref,
+    metric_ref, plan_ref, result, partial, weights, slopes, movers, keep, send1, recv1, send2, recv2, send3, recv3,
+    load_sem, x_send, x_recv, h_send, h_recv, s1_send, s1_recv, s2_send, s2_recv, s3_send, s3_recv, *fields,
 ):
     R, _, half, width = x_ref.shape
     modes = 2 * half
@@ -42,6 +42,11 @@
     def along(step):
         return (lax.rem(z + step, nz) * 2 + y) * 2 + core
 
+    load_metric = pltpu.make_async_copy(metric_hbm, metric_ref, load_sem.at[0])
+    load_plan = pltpu.make_async_copy(plan_hbm, plan_ref, load_sem.at[1])
+    load_metric.start()
+    load_plan.start()
+
     barrier = pltpu.get_barrier_semaphore()
 
     def greet(device):
@@ -68,13 +73,10 @@
             device_id=device, device_id_type=MESH,
         )
 
-    def spread(d, piece):
-        peer = (lax.rem(me + d, n_mode), s)
-        rows = ((0, 1), (R - 1, 1), (1, R - 2))[piece]
-        return remote(
-            x_ref.at[pl.ds(rows[0], rows[1])],
-            fields.at[me, pl.ds(1 + rows[0], rows[1])],
-            x_send.at[d, piece], x_recv.at[d, piece], peer,
+    def spread(d, row):
+        return remote(
+            x_ref.at[row], fields[1 + row].at[me],
+            x_send.at[d, row], x_recv.at[d, row], (lax.rem(me + d, n_mode), s),
         )
 
     def halo(d, side):
@@ -82,73 +84,76 @@
         if d == 0:
             src = x_ref.at[0 if side == 0 else R - 1]
         else:
-            src = fields.at[group, 1 if side == 0 else R]
+            src = fields[1 if side == 0 else R].at[group]
         target = (me, jnp.maximum(s - 1, 0)) if side == 0 else (me, jnp.minimum(s + 1, n - 1))
         return remote(
-            src, fields.at[group, R + 1 if side == 0 else 0],
+            src, fields[R + 1 if side == 0 else 0].at[group],
             h_send.at[d, side], h_recv.at[d, side], target,
         )
 
-    for piece in range(3):
+    for row in range(R):
         for d in range(1, n_mode):
-            spread(d, piece).start()
-
-    def start_halo(d):
-        @pl.when(has_left)
-        def _():
-            halo(d, 0).start()
-
-        @pl.when(has_right)
-        def _():
-            halo(d, 1).start()
-
-    start_halo(0)
+            spread(d, row).start()
+
+    def start_halo(d, side):
+        @pl.when(has_left if side == 0 else has_right)
+        def _():
+            halo(d, side).start()
+
+    start_halo(0, 0)
+    start_halo(0, 1)
     for r in range(R):
-        fields[me, 1 + r] = x_ref[r]
+        fields[1 + r][me] = x_ref[r]
 
     @pl.when(jnp.logical_not(has_left))
     def _():
         for g in range(n_mode):
-            fields[g, 0] = jnp.zeros_like(fields[g, 0])
+            fields[0][g] = jnp.zeros_like(fields[0][g])
 
     @pl.when(jnp.logical_not(has_right))
     def _():
         for g in range(n_mode):
-            fields[g, R + 1] = jnp.zeros_like(fields[g, R + 1])
-
-    for d in range(1, n_mode):
-        spread(d, 0).wait_recv()
-        spread(d, 1).wait_recv()
-        start_halo(d)
-    for d in range(1, n_mode):
-        spread(d, 2).wait_recv()
-    for d in range(n_mode):
-        @pl.when(has_right)
-        def _():
-            halo(d, 0).wait_recv()
-
-        @pl.when(has_left)
-        def _():
-            halo(d, 1).wait_recv()
+            fields[R + 1][g] = jnp.zeros_like(fields[R + 1][g])
+
+    load_metric.wait()
+    load_plan.wait()
+
+    def arrive(row):
+        for d in range(1, n_mode):
+            spread(d, row).wait_recv()
+            if row == 0:
+                start_halo(d, 0)
+            if row == R - 1:
+                start_halo(d, 1)
+
+    def arrive_halo():
+        for d in range(n_mode):
+            @pl.when(has_right)
+            def _():
+                halo(d, 0).wait_recv()
+
+            @pl.when(has_left)
+            def _():
+                halo(d, 1).wait_recv()
 
     lane = lax.rem(lax.broadcasted_iota(jnp.int32, (half, width), 1), L)
-    for b in range(2):
-        owner, which = plan_ref[0, b], plan_ref[1, b]
-        for r in range(R):
-            block = fields[owner, 1 + r, which].astype(F32)
+
+    def prepare(r):
+        for b in range(2):
+            owner, which = plan_ref[0, b], plan_ref[1, b]
+            block = fields[1 + r][owner, which].astype(F32)
             weight = metric_ref[2, r : r + 1, :]
             for c in range(2):
                 scaled = block[:, c * L : (c + 1) * L] * weight
                 movers[c, r, pl.ds(b * (half // jb), half // jb)] = scaled.reshape(
                     half // jb, jb, L
                 )
-    for b in range(2 // parts):
-        source = 2 + b if parts == 1 else 2 + me
-        owner, which = plan_ref[0, source], plan_ref[1, source]
-        for r in range(R):
-            low = fields[owner, r, which].astype(F32)
-            mid = fields[owner, r + 1, which].astype(F32)
-            high = fields[owner, r + 2, which].astype(F32)
+        for b in range(2 // parts):
+            source = 2 + b if parts == 1 else 2 + me
+            owner, which = plan_ref[0, source], plan_ref[1, source]
+            low = fields[r][owner, which].astype(F32)
+            mid = fields[r + 1][owner, which].astype(F32)
+            high = fields[r + 2][owner, which].astype(F32)
             first = jnp.concatenate([metric_ref[0, r : r + 1, :]] * C, axis=1)
             second = jnp.concatenate([metric_ref[1, r : r + 1, :]] * C, axis=1)
             after = jnp.where(lane == L - 1, 0.0, pltpu.roll(mid, width - 1, 1))
@@ -156,20 +161,18 @@
             place = slice(b * half, (b + 1) * half)
             slopes[0, r, place, :] = ((high - low) * first).astype(BF16).astype(F32)
             slopes[1, r, place, :] = ((after - before) * second).astype(BF16).astype(F32)
-    for r in range(R):
         if parts == 1:
             tests = x_ref[r].reshape(modes, width)
         else:
             tests = jnp.concatenate(
-                [fields[g, 1 + r].reshape(modes, width) for g in range(n_mode)], axis=0
+                [fields[1 + r][g].reshape(modes, width) for g in range(n_mode)], axis=0
             )
         weights[r] = tests.T
 
     tile = 16
 
-    def project(q):
-        total = None
-        for r in range(R):
+    def project(q, some_rows, total=None):
+        for r in some_rows:
             m = [
                 [jnp.broadcast_to(movers[d, r, q, j : j + 1, :], (tile, L)) for j in range(jb)]
                 for d in range(2)
@@ -188,6 +191,9 @@
                 jnp.concatenate(rows, axis=0), weights[r], preferred_element_type=F32
             )
             total = part if total is None else total + part
+        return total
+
+    def sort(total):
         order = [total[(k * jb + j) * tile : (k * jb + j + 1) * tile]
                  for j in range(jb) for k in range(own // tile)]
         return jnp.concatenate(order, axis=0)
@@ -226,7 +232,7 @@
         t = lax.rem(it, nz)
         column = jnp.where(it < nz, 1 - y, y)
         q = lax.rem(z + 1 + t, nz) * 2 + column
-        total = project(q)
+        total = sort(project(q, (0, R - 1), partial[q]))
         rows = total.shape[0] // 2
         low, high = total[:rows], total[rows:]
         if parts == 1:
@@ -252,6 +258,20 @@
 
         return carry
 
+    inner = range(1, R - 1)
+    for r in range(R):
+        arrive(r)
+        ready = [r - 1] if r - 1 in inner else []
+        for i in ready:
+            prepare(i)
+
+            @pl.loop(0, nq)
+            def _(q):
+                partial[q] = project(q, (i,), partial[q] if i > 1 else None)
+
+    arrive_halo()
+    prepare(0)
+    prepare(R - 1)
     lax.fori_loop(0, nq, step, 0)
 
     value = gathered(nq - 1)
@@ -270,18 +290,20 @@
         halves = [value[:, :modes], value[:, modes:]]
         if parts == 1:
             h = value.shape[0]
-            out_ref[pl.ds(0, h), :] = halves[0]
-            out_ref[pl.ds(h, h), :] = halves[1]
+            result[pl.ds(0, h), :] = halves[0]
+            result[pl.ds(h, h), :] = halves[1]
         else:
             value = jnp.concatenate(halves, axis=0)
             column = me if e == 0 else 1 - me
             for j in range(value.shape[0] // own):
                 start = pl.multiple_of(j * modes + column * own, own)
-                out_ref[pl.ds(start, own), :] = value[j * own : (j + 1) * own]
+                result[pl.ds(start, own), :] = value[j * own : (j + 1) * own]
+
+    out_ref[...] = result[...].T
 
     for d in range(1, n_mode):
-        for piece in range(3):
-            spread(d, piece).wait_send()
+        for row in range(R):
+            spread(d, row).wait_send()
     for d in range(n_mode):
         @pl.when(has_left)
         def _():
@@ -314,15 +336,18 @@
     dma = pltpu.SemaphoreType.DMA
     return pl.pallas_call(
         functools.partial(kernel, n_mode, n, parts, norm_factor),
-        out_shape=jax.ShapeDtypeStruct((out_rows, modes), F32),
+        out_shape=jax.ShapeDtypeStruct((modes, out_rows), F32),
         in_specs=[
             pl.BlockSpec(memory_space=pltpu.VMEM),
-            pl.BlockSpec(memory_space=pltpu.VMEM),
-            pl.BlockSpec(memory_space=pltpu.SMEM),
+            pl.BlockSpec(memory_space=pltpu.HBM),
+            pl.BlockSpec(memory_space=pltpu.HBM),
         ],
         out_specs=pl.BlockSpec(memory_space=pltpu.VMEM),
         scratch_shapes=[
-            pltpu.VMEM((n_mode, R + 2, 2, half, width), BF16),
+            pltpu.VMEM(metric.shape, F32),
+            pltpu.SMEM(plan.shape[::-1], jnp.int32),
+            pltpu.VMEM((out_rows, modes), F32),
+            pltpu.VMEM((nq, jb * modes // parts, modes * parts), F32),
             pltpu.VMEM((R, width, modes * parts), BF16),
             pltpu.VMEM((2, R, modes // parts, width), F32),
             pltpu.VMEM((2, R, nq, jb, L), F32),
@@ -333,8 +358,9 @@
             pltpu.VMEM((nz, h, 2 * modes), BF16),
             pltpu.VMEM((nz, parts, h // parts, 2 * modes), BF16),
             pltpu.VMEM((nz, parts, h // parts, 2 * modes), BF16),
-            dma((n_mode, 3)),
-            dma((n_mode, 3)),
+            dma((2,)),
+            dma((n_mode, R)),
+            dma((n_mode, R)),
             dma((n_mode, 2)),
             dma((n_mode, 2)),
             dma((nq,)),
@@ -343,11 +369,12 @@
             dma((nz,)),
             dma((nz, parts)),
             dma((nz, parts)),
+            *[pltpu.VMEM((n_mode, 2, half, width), BF16) for _ in range(R + 2)],
         ],
         compiler_params=pltpu.CompilerParams(
             collective_id=0, has_side_effects=True, vmem_limit_bytes=40 * 1024 * 1024
         ),
-    )(x, metric, plan.T)
+    )(x, metric, plan.T).T
 
 
 def solution(mesh):

time: 28.2 us -> 29.3 us (1.039)
  Pallas kernels: 25.4 us -> 26.6 us
    pallas_call x1, Pallas kernels: 25.4 us -> 26.6 us  [body(): pl.pallas_call(functools.partial(kernel, n_mode, n, parts, norm_factor),...]
    pallas_call x1 -> x0, local copies, waits for them, and re-layouts: 0.71 us -> none  [body(): pl.pallas_call(functools.partial(kernel, n_mode, n, parts, norm_factor),...]
    unnamed x4 -> x5, local copies, waits for them, and re-layouts: 0.52 us -> 1.15 us
where the time goes in v3:
time: 29.3 us; the launch traced here: 29.1 us
  Pallas kernels  26.6 us (91%)
  local copies, waits for them, and re-layouts  2.47 us (8%)
    pallas_call x1, Pallas kernels, body(): pl.pallas_call(functools.partial(kernel, n_mode, n, parts, norm_factor),...  26.6 us
    unnamed x5, local copies, waits for them, and re-layouts  1.15 us
    transpose x1, local copies, waits for them, and re-layouts, body(): x = mode_fields.transpose(2, 0, 1, 3).reshape(R, 2, half, width)  1.15 us

profile of v3, /device:TPU:0, one launch (start us, length us, event | category | flops | bytes accessed | tf_op | source)
XLA Modules:
  0.0 29.1 jit_solution(5418190450201051792)
XLA Ops:
  0.0 1.2 %copy.4 = bf16[4,64,2,256]{3,2,1,0:T(2,128)(2,1)S(1)} copy(bf16[4,64,2,256]{3,0,2,1:T(4,128)(2,1)} %bitcast.5) | data formatting | bytes 524288 | tf_op jit(solution)/shard_map/transpose | solution.py:335
  1.2 0.0 copy-start
  1.2 0.0 copy-start.1
  1.2 0.2 reshape.3.x_ref
  1.4 0.5 %copy-done = f32[3,4,256]{2,1,0:T(4,128)S(1)} copy-done((f32[3,4,256]{2,1,0:T(4,128)S(1)}, f32[3,4,256]{2,1,0:T(4,128)}, u32[]{:S(2)}) %copy-start) | copy-done | bytes 12312
  1.9 0.0 copy-done.1
  1.9 26.6 %shard_map.37 = f32[64,256]{1,0:T(8,128)S(1)} custom-call(bf16[4,2,32,512]{3,2,1,0:T(8,128)(2,1)S(1)} %reshape.3.x_ref, f32[3,4,256]{2,1,0:T(4,128)S(1)} %copy-done, s32[2,4]{1,0:T(2,128)S(1)} %bitcast.4), custom_call_target="tpu_custom_call" | custom-call | tf_op jit(solution)/shard_map/pallas_call | solution.py:337
  28.4 0.6 %copy.6 = f32[256,64]{0,1:T(8,128)} copy(f32[256,64]{0,1:T(8,128)S(1)} %bitcast.3) | data formatting | bytes 131072
Async XLA Ops:
  1.2 0.7 %copy-start = (f32[3,4,256]{2,1,0:T(4,128)S(1)}, f32[3,4,256]{2,1,0:T(4,128)}, u32[]{:S(2)}) copy-start(f32[3,4,256]{2,1,0:T(4,128)} %metric_hbm.1) | copy-start | bytes 36868
  1.2 0.7 %copy-start.1 = (s32[4,2]{0,1:T(2,128)S(1)}, s32[4,2]{0,1:T(2,128)}, u32[]{:S(2)}) copy-start(s32[4,2]{0,1:T(2,128)} %param.5) | copy-start | bytes 100

commit v4 on v3

--- a/solution.py
+++ b/solution.py
@@ -15,7 +15,7 @@
 def kernel(
     n_mode, n, parts, norm_factor,
     x_ref, metric_hbm, plan_hbm, out_ref,
-    metric_ref, plan_ref, result, partial, weights, slopes, movers, keep, send1, recv1, send2, recv2, send3, recv3,
+    metric_ref, plan_ref, result, weights, slopes, movers, keep, send1, recv1, send2, recv2, send3, recv3,
     load_sem, x_send, x_recv, h_send, h_recv, s1_send, s1_recv, s2_send, s2_recv, s3_send, s3_recv, *fields,
 ):
     R, _, half, width = x_ref.shape
@@ -91,7 +91,8 @@
             h_send.at[d, side], h_recv.at[d, side], target,
         )
 
-    for row in range(R):
+    arrivals = [0, R - 1] + list(range(1, R - 1))
+    for row in arrivals:
         for d in range(1, n_mode):
             spread(d, row).start()
 
@@ -161,6 +162,8 @@
             place = slice(b * half, (b + 1) * half)
             slopes[0, r, place, :] = ((high - low) * first).astype(BF16).astype(F32)
             slopes[1, r, place, :] = ((after - before) * second).astype(BF16).astype(F32)
+
+    def weigh(r):
         if parts == 1:
             tests = x_ref[r].reshape(modes, width)
         else:
@@ -228,11 +231,16 @@
         to_twin(it).wait_recv()
         return keep[it] + recv1[it].astype(F32)
 
+    def place(it):
+        even = (lax.rem(it, 2) == 0) & (it > 0)
+        t = jnp.where(even, it // 2 - 1, jnp.minimum((it + 1) // 2, nz - 1))
+        return even | (it == nq - 1), t
+
     def step(it, carry):
-        t = lax.rem(it, nz)
-        column = jnp.where(it < nz, 1 - y, y)
+        mine, t = place(it)
+        column = jnp.where(mine, y, 1 - y)
         q = lax.rem(z + 1 + t, nz) * 2 + column
-        total = sort(project(q, (0, R - 1), partial[q]))
+        total = sort(project(q, range(R)))
         rows = total.shape[0] // 2
         low, high = total[:rows], total[rows:]
         if parts == 1:
@@ -241,34 +249,28 @@
         send1[it] = jnp.where(core == 0, high, low).astype(BF16)
         to_twin(it).start()
 
-        @pl.when((it >= 1) & (it <= nz))
-        def _():
-            t = it - 1
-            send2[t] = gathered(it - 1).astype(BF16)
-            to_across(t).start()
-
-        @pl.when(it > nz)
-        def _():
-            t = it - 1 - nz
+        before, last = place(it - 1)
+
+        @pl.when((it >= 1) & jnp.logical_not(before))
+        def _():
+            send2[last] = gathered(it - 1).astype(BF16)
+            to_across(last).start()
+
+        @pl.when((it >= 1) & before)
+        def _():
             value = gathered(it - 1)
-            to_across(t).wait_recv()
-            for e, piece in enumerate(columns(value + recv2[t].astype(F32))):
-                send3[t, e] = piece.astype(BF16)
-                to_along(t, e).start()
+            to_across(last).wait_recv()
+            for e, piece in enumerate(columns(value + recv2[last].astype(F32))):
+                send3[last, e] = piece.astype(BF16)
+                to_along(last, e).start()
 
         return carry
 
-    inner = range(1, R - 1)
-    for r in range(R):
+    for r in arrivals:
         arrive(r)
-        ready = [r - 1] if r - 1 in inner else []
-        for i in ready:
-            prepare(i)
-
-            @pl.loop(0, nq)
-            def _(q):
-                partial[q] = project(q, (i,), partial[q] if i > 1 else None)
-
+        weigh(r)
+    for r in range(1, R - 1):
+        prepare(r)
     arrive_halo()
     prepare(0)
     prepare(R - 1)
@@ -347,7 +349,6 @@
             pltpu.VMEM(metric.shape, F32),
             pltpu.SMEM(plan.shape[::-1], jnp.int32),
             pltpu.VMEM((out_rows, modes), F32),
-            pltpu.VMEM((nq, jb * modes // parts, modes * parts), F32),
             pltpu.VMEM((R, width, modes * parts), BF16),
             pltpu.VMEM((2, R, modes // parts, width), F32),
             pltpu.VMEM((2, R, nq, jb, L), F32),

time: 29.3 us -> 29.3 us (level)
  no operation moved by 1% of the time
where the time goes in v4:
time: 29.3 us; the launch traced here: 29 us
  Pallas kernels  26.5 us (90%)
  local copies, waits for them, and re-layouts  2.47 us (8%)
    pallas_call x1, Pallas kernels, body(): pl.pallas_call(functools.partial(kernel, n_mode, n, parts, norm_factor),...  26.5 us
    transpose x1, local copies, waits for them, and re-layouts, body(): x = mode_fields.transpose(2, 0, 1, 3).reshape(R, 2, half, width)  1.15 us
    unnamed x5, local copies, waits for them, and re-layouts  1.15 us

profile of v4, /device:TPU:0, one launch (start us, length us, event | category | flops | bytes accessed | tf_op | source)
XLA Modules:
  0.0 29.0 jit_solution(16581422560655361648)
XLA Ops:
  0.0 1.2 %copy.4 = bf16[4,64,2,256]{3,2,1,0:T(2,128)(2,1)S(1)} copy(bf16[4,64,2,256]{3,0,2,1:T(4,128)(2,1)} %bitcast.5) | data formatting | bytes 524288 | tf_op jit(solution)/shard_map/transpose | solution.py:337
  1.2 0.0 copy-start
  1.2 0.0 copy-start.1
  1.2 0.2 reshape.3.x_ref
  1.4 0.5 %copy-done = f32[3,4,256]{2,1,0:T(4,128)S(1)} copy-done((f32[3,4,256]{2,1,0:T(4,128)S(1)}, f32[3,4,256]{2,1,0:T(4,128)}, u32[]{:S(2)}) %copy-start) | copy-done | bytes 12312
  1.9 0.0 copy-done.1
  1.9 26.5 %shard_map.37 = f32[64,256]{1,0:T(8,128)S(1)} custom-call(bf16[4,2,32,512]{3,2,1,0:T(8,128)(2,1)S(1)} %reshape.3.x_ref, f32[3,4,256]{2,1,0:T(4,128)S(1)} %copy-done, s32[2,4]{1,0:T(2,128)S(1)} %bitcast.4), custom_call_target="tpu_custom_call" | custom-call | tf_op jit(solution)/shard_map/pallas_call | solution.py:339
  28.4 0.6 %copy.6 = f32[256,64]{0,1:T(8,128)} copy(f32[256,64]{0,1:T(8,128)S(1)} %bitcast.3) | data formatting | bytes 131072
Async XLA Ops:
  1.2 0.7 %copy-start = (f32[3,4,256]{2,1,0:T(4,128)S(1)}, f32[3,4,256]{2,1,0:T(4,128)}, u32[]{:S(2)}) copy-start(f32[3,4,256]{2,1,0:T(4,128)} %metric_hbm.1) | copy-start | bytes 36868
  1.2 0.7 %copy-start.1 = (s32[4,2]{0,1:T(2,128)S(1)}, s32[4,2]{0,1:T(2,128)}, u32[]{:S(2)}) copy-start(s32[4,2]{0,1:T(2,128)} %param.5) | copy-start | bytes 100

commit v5 on v4

--- a/solution.py
+++ b/solution.py
@@ -231,14 +231,23 @@
         to_twin(it).wait_recv()
         return keep[it] + recv1[it].astype(F32)
 
-    def place(it):
-        even = (lax.rem(it, 2) == 0) & (it > 0)
-        t = jnp.where(even, it // 2 - 1, jnp.minimum((it + 1) // 2, nz - 1))
-        return even | (it == nq - 1), t
+    lag = min(3, nz)
+
+    def forward_across(it):
+        send2[it] = gathered(it).astype(BF16)
+        to_across(it).start()
+
+    def forward_along(it):
+        t = it - nz
+        value = gathered(it)
+        to_across(t).wait_recv()
+        for e, piece in enumerate(columns(value + recv2[t].astype(F32))):
+            send3[t, e] = piece.astype(BF16)
+            to_along(t, e).start()
 
     def step(it, carry):
-        mine, t = place(it)
-        column = jnp.where(mine, y, 1 - y)
+        t = lax.rem(it, nz)
+        column = jnp.where(it < nz, 1 - y, y)
         q = lax.rem(z + 1 + t, nz) * 2 + column
         total = sort(project(q, range(R)))
         rows = total.shape[0] // 2
@@ -249,20 +258,13 @@
         send1[it] = jnp.where(core == 0, high, low).astype(BF16)
         to_twin(it).start()
 
-        before, last = place(it - 1)
-
-        @pl.when((it >= 1) & jnp.logical_not(before))
-        def _():
-            send2[last] = gathered(it - 1).astype(BF16)
-            to_across(last).start()
-
-        @pl.when((it >= 1) & before)
-        def _():
-            value = gathered(it - 1)
-            to_across(last).wait_recv()
-            for e, piece in enumerate(columns(value + recv2[last].astype(F32))):
-                send3[last, e] = piece.astype(BF16)
-                to_along(last, e).start()
+        @pl.when((it >= lag) & (it < lag + nz))
+        def _():
+            forward_across(it - lag)
+
+        @pl.when(it >= lag + nz)
+        def _():
+            forward_along(it - lag)
 
         return carry
 
@@ -275,6 +277,8 @@
     prepare(0)
     prepare(R - 1)
     lax.fori_loop(0, nq, step, 0)
+    for it in range(nq - lag, nq - 1):
+        forward_along(it)
 
     value = gathered(nq - 1)
     to_across(nz - 1).wait_recv()

time: 29.3 us -> 27 us (0.922)
  Pallas kernels: 26.5 us -> 24.2 us
    pallas_call x1, Pallas kernels: 26.5 us -> 24.2 us  [body(): pl.pallas_call(functools.partial(kernel, n_mode, n, parts, norm_factor),...]
where the time goes in v5:
time: 27 us; the launch traced here: 26.7 us
  Pallas kernels  24.2 us (90%)
  local copies, waits for them, and re-layouts  2.47 us (9%)
    pallas_call x1, Pallas kernels, body(): pl.pallas_call(functools.partial(kernel, n_mode, n, parts, norm_factor),...  24.2 us
    transpose x1, local copies, waits for them, and re-layouts, body(): x = mode_fields.transpose(2, 0, 1, 3).reshape(R, 2, half, width)  1.15 us
    unnamed x5, local copies, waits for them, and re-layouts  1.15 us

profile of v5, /device:TPU:0, one launch (start us, length us, event | category | flops | bytes accessed | tf_op | source)
XLA Modules:
  0.0 26.7 jit_solution(521613736898445173)
XLA Ops:
  0.0 1.2 %copy.4 = bf16[4,64,2,256]{3,2,1,0:T(2,128)(2,1)S(1)} copy(bf16[4,64,2,256]{3,0,2,1:T(4,128)(2,1)} %bitcast.5) | data formatting | bytes 524288 | tf_op jit(solution)/shard_map/transpose | solution.py:341
  1.2 0.0 copy-start
  1.2 0.0 copy-start.1
  1.2 0.2 reshape.3.x_ref
  1.4 0.5 %copy-done = f32[3,4,256]{2,1,0:T(4,128)S(1)} copy-done((f32[3,4,256]{2,1,0:T(4,128)S(1)}, f32[3,4,256]{2,1,0:T(4,128)}, u32[]{:S(2)}) %copy-start) | copy-done | bytes 12312
  1.9 0.0 copy-done.1
  1.9 24.2 %shard_map.37 = f32[64,256]{1,0:T(8,128)S(1)} custom-call(bf16[4,2,32,512]{3,2,1,0:T(8,128)(2,1)S(1)} %reshape.3.x_ref, f32[3,4,256]{2,1,0:T(4,128)S(1)} %copy-done, s32[2,4]{1,0:T(2,128)S(1)} %bitcast.4), custom_call_target="tpu_custom_call" | custom-call | tf_op jit(solution)/shard_map/pallas_call | solution.py:343
  26.1 0.6 %copy.6 = f32[256,64]{0,1:T(8,128)} copy(f32[256,64]{0,1:T(8,128)S(1)} %bitcast.3) | data formatting | bytes 131072
Async XLA Ops:
  1.2 0.7 %copy-start = (f32[3,4,256]{2,1,0:T(4,128)S(1)}, f32[3,4,256]{2,1,0:T(4,128)}, u32[]{:S(2)}) copy-start(f32[3,4,256]{2,1,0:T(4,128)} %metric_hbm.1) | copy-start | bytes 36868
  1.2 0.7 %copy-start.1 = (s32[4,2]{0,1:T(2,128)S(1)}, s32[4,2]{0,1:T(2,128)}, u32[]{:S(2)}) copy-start(s32[4,2]{0,1:T(2,128)} %param.5) | copy-start | bytes 100

commit v6 on v5

--- a/solution.py
+++ b/solution.py
@@ -15,14 +15,13 @@
 def kernel(
     n_mode, n, parts, norm_factor,
     x_ref, metric_hbm, plan_hbm, out_ref,
-    metric_ref, plan_ref, result, weights, slopes, movers, keep, send1, recv1, send2, recv2, send3, recv3,
+    metric_ref, plan_ref, result, partial, weights, slopes, movers, keep, send1, recv1, send2, recv2, send3, recv3,
     load_sem, x_send, x_recv, h_send, h_recv, s1_send, s1_recv, s2_send, s2_recv, s3_send, s3_recv, *fields,
 ):
-    R, _, half, width = x_ref.shape
+    R, C, _, half, L = x_ref.shape
+    width = C * L
     modes = 2 * half
     own = modes // parts
-    L = metric_ref.shape[2]
-    C = width // L
     nq, nz = n // 2, n // 4
     jb = movers.shape[3]
 
@@ -137,40 +136,40 @@
             def _():
                 halo(d, 1).wait_recv()
 
-    lane = lax.rem(lax.broadcasted_iota(jnp.int32, (half, width), 1), L)
+    lane = lax.broadcasted_iota(jnp.int32, (half, L), 1)
 
     def prepare(r):
+        first, second, weight = (metric_ref[i, r : r + 1, :] for i in range(3))
         for b in range(2):
             owner, which = plan_ref[0, b], plan_ref[1, b]
-            block = fields[1 + r][owner, which].astype(F32)
-            weight = metric_ref[2, r : r + 1, :]
             for c in range(2):
-                scaled = block[:, c * L : (c + 1) * L] * weight
+                scaled = fields[1 + r][owner, c, which].astype(F32) * weight
                 movers[c, r, pl.ds(b * (half // jb), half // jb)] = scaled.reshape(
                     half // jb, jb, L
                 )
         for b in range(2 // parts):
             source = 2 + b if parts == 1 else 2 + me
             owner, which = plan_ref[0, source], plan_ref[1, source]
-            low = fields[r][owner, which].astype(F32)
-            mid = fields[r + 1][owner, which].astype(F32)
-            high = fields[r + 2][owner, which].astype(F32)
-            first = jnp.concatenate([metric_ref[0, r : r + 1, :]] * C, axis=1)
-            second = jnp.concatenate([metric_ref[1, r : r + 1, :]] * C, axis=1)
-            after = jnp.where(lane == L - 1, 0.0, pltpu.roll(mid, width - 1, 1))
-            before = jnp.where(lane == 0, 0.0, pltpu.roll(mid, 1, 1))
-            place = slice(b * half, (b + 1) * half)
-            slopes[0, r, place, :] = ((high - low) * first).astype(BF16).astype(F32)
-            slopes[1, r, place, :] = ((after - before) * second).astype(BF16).astype(F32)
+            rows = slice(b * half, (b + 1) * half)
+            for c in range(C):
+                lanes = slice(c * L, (c + 1) * L)
+                low = fields[r][owner, c, which].astype(F32)
+                mid = fields[r + 1][owner, c, which].astype(F32)
+                high = fields[r + 2][owner, c, which].astype(F32)
+                after = jnp.where(lane == L - 1, 0.0, pltpu.roll(mid, L - 1, 1))
+                before = jnp.where(lane == 0, 0.0, pltpu.roll(mid, 1, 1))
+                slopes[0, r, rows, lanes] = ((high - low) * first).astype(BF16).astype(F32)
+                slopes[1, r, rows, lanes] = ((after - before) * second).astype(BF16).astype(F32)
 
     def weigh(r):
-        if parts == 1:
-            tests = x_ref[r].reshape(modes, width)
-        else:
-            tests = jnp.concatenate(
-                [fields[1 + r][g].reshape(modes, width) for g in range(n_mode)], axis=0
-            )
-        weights[r] = tests.T
+        for c in range(C):
+            if parts == 1:
+                tests = x_ref[r, c].reshape(modes, L)
+            else:
+                tests = jnp.concatenate(
+                    [fields[1 + r][g, c].reshape(modes, L) for g in range(n_mode)], axis=0
+                )
+            weights[r, c * L : (c + 1) * L, :] = tests.T
 
     tile = 16
 
@@ -249,7 +248,7 @@
         t = lax.rem(it, nz)
         column = jnp.where(it < nz, 1 - y, y)
         q = lax.rem(z + 1 + t, nz) * 2 + column
-        total = sort(project(q, range(R)))
+        total = sort(project(q, (0, R - 1), partial[q]))
         rows = total.shape[0] // 2
         low, high = total[:rows], total[rows:]
         if parts == 1:
@@ -273,6 +272,11 @@
         weigh(r)
     for r in range(1, R - 1):
         prepare(r)
+
+    @pl.loop(0, nq)
+    def _(q):
+        partial[q] = project(q, range(1, R - 1))
+
     arrive_halo()
     prepare(0)
     prepare(R - 1)
@@ -338,7 +342,7 @@
     nq, nz = n // 2, n // 4
     jb = modes // nq
     parts = 2 if n_mode == 2 else 1
-    x = mode_fields.transpose(2, 0, 1, 3).reshape(R, 2, half, width)
+    x = mode_fields.transpose(2, 1, 0, 3).reshape(R, C, 2, half, L)
     dma = pltpu.SemaphoreType.DMA
     return pl.pallas_call(
         functools.partial(kernel, n_mode, n, parts, norm_factor),
@@ -353,6 +357,7 @@
             pltpu.VMEM(metric.shape, F32),
             pltpu.SMEM(plan.shape[::-1], jnp.int32),
             pltpu.VMEM((out_rows, modes), F32),
+            pltpu.VMEM((nq, jb * modes // parts, modes * parts), F32),
             pltpu.VMEM((R, width, modes * parts), BF16),
             pltpu.VMEM((2, R, modes // parts, width), F32),
             pltpu.VMEM((2, R, nq, jb, L), F32),
@@ -374,7 +379,7 @@
             dma((nz,)),
             dma((nz, parts)),
             dma((nz, parts)),
-            *[pltpu.VMEM((n_mode, 2, half, width), BF16) for _ in range(R + 2)],
+            *[pltpu.VMEM((n_mode, C, 2, half, L), BF16) for _ in range(R + 2)],
         ],
         compiler_params=pltpu.CompilerParams(
             collective_id=0, has_side_effects=True, vmem_limit_bytes=40 * 1024 * 1024

time: 27 us -> 28.6 us (1.059)
  Pallas kernels: 24.2 us -> 26.1 us
    pallas_call x1, Pallas kernels: 24.2 us -> 26.1 us  [body(): pl.pallas_call(functools.partial(kernel, n_mode, n, parts, norm_factor),...]
where the time goes in v6:
time: 28.6 us; the launch traced here: 28.5 us
  Pallas kernels  26.1 us (91%)
  local copies, waits for them, and re-layouts  2.31 us (8%)
    pallas_call x1, Pallas kernels, body(): pl.pallas_call(functools.partial(kernel, n_mode, n, parts, norm_factor),...  26.1 us
    unnamed x5, local copies, waits for them, and re-layouts  1.3 us
    transpose x1, local copies, waits for them, and re-layouts, body(): x = mode_fields.transpose(2, 1, 0, 3).reshape(R, C, 2, half, L)  1.01 us

profile of v6, /device:TPU:0, one launch (start us, length us, event | category | flops | bytes accessed | tf_op | source)
XLA Modules:
  0.0 28.5 jit_solution(2414376152700434452)
XLA Ops:
  0.0 0.0 copy-start
  0.0 1.0 %copy.4 = bf16[4,2,64,256]{3,2,1,0:T(8,128)(2,1)S(1)} copy(bf16[4,2,64,256]{3,0,1,2:T(4,128)(2,1)} %bitcast.7) | data formatting | bytes 524288 | tf_op jit(solution)/shard_map/transpose | solution.py:345
  1.0 0.0 copy-start.1
  1.0 0.0 copy-done
  1.0 0.7 %copy-done.1 = s32[4,2]{0,1:T(2,128)S(1)} copy-done((s32[4,2]{0,1:T(2,128)S(1)}, s32[4,2]{0,1:T(2,128)}, u32[]{:S(2)}) %copy-start.1) | copy-done | bytes 56
  1.7 26.1 %shard_map.37 = f32[64,256]{1,0:T(8,128)S(1)} custom-call(bf16[4,2,2,32,256]{4,3,2,1,0:T(8,128)(2,1)S(1)} %bitcast.4, f32[3,4,256]{2,1,0:T(4,128)S(1)} %copy-done, s32[2,4]{1,0:T(2,128)S(1)} %bitcast.6), custom_call_target="tpu_custom_call" | custom-call | tf_op jit(solution)/shard_map/pallas_call | solution.py:347
  27.8 0.6 %copy.6 = f32[256,64]{0,1:T(8,128)} copy(f32[256,64]{0,1:T(8,128)S(1)} %bitcast.5) | data formatting | bytes 131072
Async XLA Ops:
  0.0 1.0 %copy-start = (f32[3,4,256]{2,1,0:T(4,128)S(1)}, f32[3,4,256]{2,1,0:T(4,128)}, u32[]{:S(2)}) copy-start(f32[3,4,256]{2,1,0:T(4,128)} %metric_hbm.1) | copy-start | bytes 36868
  1.0 0.7 %copy-start.1 = (s32[4,2]{0,1:T(2,128)S(1)}, s32[4,2]{0,1:T(2,128)}, u32[]{:S(2)}) copy-start(s32[4,2]{0,1:T(2,128)} %param.5) | copy-start | bytes 100

commit v7 on v6

--- a/solution.py
+++ b/solution.py
@@ -14,8 +14,8 @@
 
 def kernel(
     n_mode, n, parts, norm_factor,
-    x_ref, metric_hbm, plan_hbm, out_ref,
-    metric_ref, plan_ref, result, partial, weights, slopes, movers, keep, send1, recv1, send2, recv2, send3, recv3,
+    raw_ref, metric_hbm, plan_hbm, out_ref,
+    metric_ref, plan_ref, result, x_ref, weights, slopes, movers, keep, send1, recv1, send2, recv2, send3, recv3,
     load_sem, x_send, x_recv, h_send, h_recv, s1_send, s1_recv, s2_send, s2_recv, s3_send, s3_recv, *fields,
 ):
     R, C, _, half, L = x_ref.shape
@@ -62,6 +62,11 @@
     @pl.when(has_other)
     def _():
         greet((me, other))
+
+    for c in range(C):
+        turned = jnp.swapaxes(raw_ref[:, c].astype(F32), 0, 1)
+        for r in range(R):
+            x_ref[r, c] = turned[r].astype(BF16).reshape(2, half, L)
 
     greeted = (n_mode - 1) + 2 + parts * (nz - 1)
     pl.semaphore_wait(barrier, jnp.where(has_other, greeted + 1, greeted))
@@ -248,7 +253,7 @@
         t = lax.rem(it, nz)
         column = jnp.where(it < nz, 1 - y, y)
         q = lax.rem(z + 1 + t, nz) * 2 + column
-        total = sort(project(q, (0, R - 1), partial[q]))
+        total = sort(project(q, range(R)))
         rows = total.shape[0] // 2
         low, high = total[:rows], total[rows:]
         if parts == 1:
@@ -272,11 +277,6 @@
         weigh(r)
     for r in range(1, R - 1):
         prepare(r)
-
-    @pl.loop(0, nq)
-    def _(q):
-        partial[q] = project(q, range(1, R - 1))
-
     arrive_halo()
     prepare(0)
     prepare(R - 1)
@@ -342,7 +342,6 @@
     nq, nz = n // 2, n // 4
     jb = modes // nq
     parts = 2 if n_mode == 2 else 1
-    x = mode_fields.transpose(2, 1, 0, 3).reshape(R, C, 2, half, L)
     dma = pltpu.SemaphoreType.DMA
     return pl.pallas_call(
         functools.partial(kernel, n_mode, n, parts, norm_factor),
@@ -357,7 +356,7 @@
             pltpu.VMEM(metric.shape, F32),
             pltpu.SMEM(plan.shape[::-1], jnp.int32),
             pltpu.VMEM((out_rows, modes), F32),
-            pltpu.VMEM((nq, jb * modes // parts, modes * parts), F32),
+            pltpu.VMEM((R, C, 2, half, L), BF16),
             pltpu.VMEM((R, width, modes * parts), BF16),
             pltpu.VMEM((2, R, modes // parts, width), F32),
             pltpu.VMEM((2, R, nq, jb, L), F32),
@@ -384,7 +383,7 @@
         compiler_params=pltpu.CompilerParams(
             collective_id=0, has_side_effects=True, vmem_limit_bytes=40 * 1024 * 1024
         ),
-    )(x, metric, plan.T).T
+    )(mode_fields, metric, plan.T).T
 
 
 def solution(mesh):

time: 28.6 us -> 27.4 us (0.958)
  Pallas kernels: 26.1 us -> 24.2 us
  local copies, waits for them, and re-layouts: 2.31 us -> 2.97 us
    pallas_call x1, Pallas kernels: 26.1 us -> 24.2 us  [body(): pl.pallas_call(functools.partial(kernel, n_mode, n, parts, norm_factor),...]
    unnamed x5 -> x7, local copies, waits for them, and re-layouts: 1.3 us -> 2.97 us
    transpose x1 -> x0, local copies, waits for them, and re-layouts: 1.01 us -> none  [body(): x = mode_fields.transpose(2, 1, 0, 3).reshape(R, C, 2, half, L)]
where the time goes in v7:
time: 27.4 us; the launch traced here: 27.2 us
  Pallas kernels  24.2 us (88%)
  local copies, waits for them, and re-layouts  2.97 us (11%)
    pallas_call x1, Pallas kernels, body(): pl.pallas_call(functools.partial(kernel, n_mode, n, parts, norm_factor),...  24.2 us
    unnamed x7, local copies, waits for them, and re-layouts  2.97 us

profile of v7, /device:TPU:0, one launch (start us, length us, event | category | flops | bytes accessed | tf_op | source)
XLA Modules:
  0.0 27.2 jit_solution(16242633651176726571)
XLA Ops:
  0.0 0.0 copy-start.2
  0.0 0.7 %copy-done.2 = s32[4,2]{0,1:T(2,128)S(1)} copy-done((s32[4,2]{0,1:T(2,128)S(1)}, s32[4,2]{0,1:T(2,128)}, u32[]{:S(2)}) %copy-start.2) | copy-done | bytes 56
  0.7 0.0 copy-start
  0.7 0.9 %copy-done = bf16[64,2,4,256]{3,2,1,0:T(4,128)(2,1)S(1)} copy-done((bf16[64,2,4,256]{3,2,1,0:T(4,128)(2,1)S(1)}, bf16[64,2,4,256]{3,2,1,0:T(4,128)(2,1)}, u32[]{:S(2)}) %copy-start) | copy-done | bytes 262168
  1.6 0.0 copy-start.1
  1.6 0.7 %copy-done.1 = f32[3,4,256]{2,1,0:T(4,128)S(1)} copy-done((f32[3,4,256]{2,1,0:T(4,128)S(1)}, f32[3,4,256]{2,1,0:T(4,128)}, u32[]{:S(2)}) %copy-start.1) | copy-done | bytes 12312
  2.3 24.2 %shard_map.37 = f32[64,256]{1,0:T(8,128)S(1)} custom-call(bf16[64,2,4,256]{3,2,1,0:T(4,128)(2,1)S(1)} %copy-done, f32[3,4,256]{2,1,0:T(4,128)S(1)} %copy-done.1, s32[2,4]{1,0:T(2,128)S(1)} %bitcast.3), custom_call_target="tpu_custom_call" | custom-call | tf_op jit(solution)/shard_map/pallas_call | solution.py:346
  26.5 0.6 %copy.5 = f32[256,64]{0,1:T(8,128)} copy(f32[256,64]{0,1:T(8,128)S(1)} %bitcast.2) | data formatting | bytes 131072
Async XLA Ops:
  0.0 0.7 %copy-start.2 = (s32[4,2]{0,1:T(2,128)S(1)}, s32[4,2]{0,1:T(2,128)}, u32[]{:S(2)}) copy-start(s32[4,2]{0,1:T(2,128)} %param.5) | copy-start | bytes 100
  0.7 0.9 %copy-start = (bf16[64,2,4,256]{3,2,1,0:T(4,128)(2,1)S(1)}, bf16[64,2,4,256]{3,2,1,0:T(4,128)(2,1)}, u32[]{:S(2)}) copy-start(bf16[64,2,4,256]{3,2,1,0:T(4,128)(2,1)} %raw_ref.1) | copy-start | bytes 786436
  1.6 0.7 %copy-start.1 = (f32[3,4,256]{2,1,0:T(4,128)S(1)}, f32[3,4,256]{2,1,0:T(4,128)}, u32[]{:S(2)}) copy-start(f32[3,4,256]{2,1,0:T(4,128)} %metric_hbm.1) | copy-start | bytes 36868

commit v8 on v7

--- a/solution.py
+++ b/solution.py
@@ -14,8 +14,8 @@
 
 def kernel(
     n_mode, n, parts, norm_factor,
-    raw_ref, metric_hbm, plan_hbm, out_ref,
-    metric_ref, plan_ref, result, x_ref, weights, slopes, movers, keep, send1, recv1, send2, recv2, send3, recv3,
+    raw_hbm, metric_hbm, plan_hbm, out_ref,
+    raw_ref, metric_ref, plan_ref, result, x_ref, weights, slopes, movers, keep, send1, recv1, send2, recv2, send3, recv3,
     load_sem, x_send, x_recv, h_send, h_recv, s1_send, s1_recv, s2_send, s2_recv, s3_send, s3_recv, *fields,
 ):
     R, C, _, half, L = x_ref.shape
@@ -43,6 +43,8 @@
 
     load_metric = pltpu.make_async_copy(metric_hbm, metric_ref, load_sem.at[0])
     load_plan = pltpu.make_async_copy(plan_hbm, plan_ref, load_sem.at[1])
+    load_raw = pltpu.make_async_copy(raw_hbm, raw_ref, load_sem.at[2])
+    load_raw.start()
     load_metric.start()
     load_plan.start()
 
@@ -63,6 +65,7 @@
     def _():
         greet((me, other))
 
+    load_raw.wait()
     for c in range(C):
         turned = jnp.swapaxes(raw_ref[:, c].astype(F32), 0, 1)
         for r in range(R):
@@ -347,12 +350,13 @@
         functools.partial(kernel, n_mode, n, parts, norm_factor),
         out_shape=jax.ShapeDtypeStruct((modes, out_rows), F32),
         in_specs=[
-            pl.BlockSpec(memory_space=pltpu.VMEM),
+            pl.BlockSpec(memory_space=pltpu.HBM),
             pl.BlockSpec(memory_space=pltpu.HBM),
             pl.BlockSpec(memory_space=pltpu.HBM),
         ],
         out_specs=pl.BlockSpec(memory_space=pltpu.VMEM),
         scratch_shapes=[
+            pltpu.VMEM(mode_fields.shape, BF16),
             pltpu.VMEM(metric.shape, F32),
             pltpu.SMEM(plan.shape[::-1], jnp.int32),
             pltpu.VMEM((out_rows, modes), F32),
@@ -367,7 +371,7 @@
             pltpu.VMEM((nz, h, 2 * modes), BF16),
             pltpu.VMEM((nz, parts, h // parts, 2 * modes), BF16),
             pltpu.VMEM((nz, parts, h // parts, 2 * modes), BF16),
-            dma((2,)),
+            dma((3,)),
             dma((n_mode, R)),
             dma((n_mode, R)),
             dma((n_mode, 2)),
@@ -381,7 +385,7 @@
             *[pltpu.VMEM((n_mode, C, 2, half, L), BF16) for _ in range(R + 2)],
         ],
         compiler_params=pltpu.CompilerParams(
-            collective_id=0, has_side_effects=True, vmem_limit_bytes=40 * 1024 * 1024
+            collective_id=0, has_side_effects=True, vmem_limit_bytes=64 * 1024 * 1024 - 192 * 1024
         ),
     )(mode_fields, metric, plan.T).T
 

time: 27.4 us -> 26.5 us (0.967)
  local copies, waits for them, and re-layouts: 2.97 us -> 1.47 us
  Pallas kernels: 24.2 us -> 24.8 us
    unnamed x7 -> x1, local copies, waits for them, and re-layouts: 2.97 us -> 1.47 us
    pallas_call x1, Pallas kernels: 24.2 us -> 24.8 us  [body(): pl.pallas_call(functools.partial(kernel, n_mode, n, parts, norm_factor),...]
where the time goes in v8:
time: 26.5 us; the launch traced here: 26.3 us
  Pallas kernels  24.8 us (94%)
  local copies, waits for them, and re-layouts  1.47 us (6%)
    pallas_call x1, Pallas kernels, body(): pl.pallas_call(functools.partial(kernel, n_mode, n, parts, norm_factor),...  24.8 us
    unnamed x1, local copies, waits for them, and re-layouts  1.47 us

profile of v8, /device:TPU:0, one launch (start us, length us, event | category | flops | bytes accessed | tf_op | source)
XLA Modules:
  0.0 26.3 jit_solution(15530208074980820118)
XLA Ops:
  0.0 24.8 %shard_map.37 = f32[64,256]{1,0:T(8,128)} custom-call(bf16[64,2,4,256]{3,2,1,0:T(4,128)(2,1)} %raw_hbm.1, f32[3,4,256]{2,1,0:T(4,128)} %metric_hbm.1, s32[2,4]{1,0:T(2,128)} %bitcast.3), custom_call_target="tpu_custom_call" | custom-call | tf_op jit(solution)/shard_map/pallas_call | solution.py:349
  24.8 1.5 %copy.5 = f32[256,64]{0,1:T(8,128)} copy(f32[256,64]{0,1:T(8,128)} %bitcast.2) | data formatting | bytes 131072

commit v9 on v8

--- a/solution.py
+++ b/solution.py
@@ -238,7 +238,7 @@
         to_twin(it).wait_recv()
         return keep[it] + recv1[it].astype(F32)
 
-    lag = min(3, nz)
+    lag = min(2, nz)
 
     def forward_across(it):
         send2[it] = gathered(it).astype(BF16)

time: 26.5 us -> 26.3 us (level)
  no operation moved by 1% of the time
where the time goes in v9:
time: 26.3 us; the launch traced here: 26.1 us
  Pallas kernels  24.7 us (94%)
  local copies, waits for them, and re-layouts  1.47 us (6%)
    pallas_call x1, Pallas kernels, body(): pl.pallas_call(functools.partial(kernel, n_mode, n, parts, norm_factor),...  24.7 us
    unnamed x1, local copies, waits for them, and re-layouts  1.47 us

profile of v9, /device:TPU:0, one launch (start us, length us, event | category | flops | bytes accessed | tf_op | source)
XLA Modules:
  0.0 26.1 jit_solution(10972925557169975045)
XLA Ops:
  0.0 24.7 %shard_map.37 = f32[64,256]{1,0:T(8,128)} custom-call(bf16[64,2,4,256]{3,2,1,0:T(4,128)(2,1)} %raw_hbm.1, f32[3,4,256]{2,1,0:T(4,128)} %metric_hbm.1, s32[2,4]{1,0:T(2,128)} %bitcast.3), custom_call_target="tpu_custom_call" | custom-call | tf_op jit(solution)/shard_map/pallas_call | solution.py:349
  24.7 1.5 %copy.5 = f32[256,64]{0,1:T(8,128)} copy(f32[256,64]{0,1:T(8,128)} %bitcast.2) | data formatting | bytes 131072
